TPU v7x, 32 devices: a whole 2x2x4 slice. The times are simulated.
32 devices in a mesh: outer: 2 (over core), row: 16 (over z, y, x).
Axes of the slice: x: 2, y: 2, z: 4, core: 2. Of those that a mesh axis runs over, the one named last changes fastest.
Arguments:
- grad_gate: bfloat16 [2, 8192, 14336], P('outer', 'row'), may hold values from -6 to 6
- grad_up: bfloat16 [2, 8192, 14336], P('outer', 'row'), may hold values from -6 to 6
- basis_gate: bfloat16 [32, 14336], P(None, 'row'), may hold values from -0.046875 to 0.046875
- basis_up: bfloat16 [32, 14336], P(None, 'row'), may hold values from -0.046875 to 0.046875
Outputs:
- next_gate: float32 [32, 14336], P(None, 'row')
- next_up: float32 [32, 14336], P(None, 'row')
- factor_gate: float32 [8192, 32], P('row')
- factor_up: float32 [8192, 32], P('row')
- resid_gate: bfloat16 [2, 8192, 14336], P('outer', 'row')
- resid_up: bfloat16 [2, 8192, 14336], P('outer', 'row')
All inputs are finite; a program needn't handle non-finite values.
Results may differ from a plain program's by a relative error of at most 0.005.
Values may be sent and summed in bfloat16 or wider, within the bound.
A program may use at most 128 MiB of HBM per device.

v0:
```python
import jax
import jax.numpy as jnp
from jax import lax
from jax.sharding import PartitionSpec as P


def forward_solve(lower_matrix, right_hand):
    return jax.scipy.linalg.solve_triangular(lower_matrix, right_hand, lower=True)


def contract_cols(left, right):
    return lax.dot_general(
        left, right, (((1,), (1,)), ((), ())), preferred_element_type=jnp.float32
    )


def contract_rows(left, right):
    return lax.dot_general(
        left, right, (((0,), (0,)), ((), ())), preferred_element_type=jnp.float32
    )


def local(grad_gate, grad_up, basis_gate, basis_up):
    pod_count = lax.axis_size("outer")
    gate_rows = grad_gate[0]
    up_rows = grad_up[0]
    full_cols = gate_rows.shape[1]
    summed = lax.psum(
        (
            contract_cols(gate_rows, lax.all_gather(basis_gate, "row", axis=1, tiled=True)),
            contract_cols(up_rows, lax.all_gather(basis_up, "row", axis=1, tiled=True)),
        ),
        "outer",
    )
    round_gate = (summed[0] / pod_count).astype(jnp.bfloat16)
    round_up = (summed[1] / pod_count).astype(jnp.bfloat16)
    gram_pair = lax.psum(
        (contract_rows(round_gate, round_gate), contract_rows(round_up, round_up)), "row"
    )
    lower_gate = jnp.linalg.cholesky(gram_pair[0])
    lower_up = jnp.linalg.cholesky(gram_pair[1])
    products = (contract_rows(round_gate, gate_rows), contract_rows(round_up, up_rows))
    shard_cols = full_cols // lax.axis_size("row")
    shard_start = lax.axis_index("row") * shard_cols
    totals = lax.psum((products[0], products[1]), ("outer", "row"))
    full_gate = forward_solve(lower_gate, totals[0] / pod_count)
    full_up = forward_solve(lower_up, totals[1] / pod_count)
    next_gate = lax.dynamic_slice_in_dim(full_gate, shard_start, shard_cols, 1)
    next_up = lax.dynamic_slice_in_dim(full_up, shard_start, shard_cols, 1)
    factor_gate = forward_solve(lower_gate, round_gate.astype(jnp.float32).T).T
    factor_up = forward_solve(lower_up, round_up.astype(jnp.float32).T).T
    resid_gate = (
        gate_rows - jnp.dot(factor_gate, full_gate, precision=lax.Precision.HIGHEST)
    ).astype(jnp.bfloat16)
    resid_up = (up_rows - jnp.dot(factor_up, full_up, precision=lax.Precision.HIGHEST)).astype(
        jnp.bfloat16
    )
    return (next_gate, next_up, factor_gate, factor_up, resid_gate[None], resid_up[None])


def solution(mesh):
    return jax.shard_map(
        local,
        mesh=mesh,
        in_specs=(P("outer", "row", None), P("outer", "row", None), P(None, "row"), P(None, "row")),
        out_specs=(
            P(None, "row"),
            P(None, "row"),
            P("row", None),
            P("row", None),
            P("outer", "row", None),
            P("outer", "row", None),
        ),
        check_vma=False,
    )
```

profile of v0, /device:TPU:1, one launch (start us, length us, event | category | flops | bytes accessed | tf_op | source)
XLA Modules:
  0.0 354.2 jit_solution(4470182728308237706)
XLA Ops:
  7.2 0.0 all-reduce.8.cloned.1.call-start
  7.2 40.6 %all_gather.6 = bf16[32,14336]{1,0:T(8,128)(2,1)S(1)} all-gather(bf16[32,896]{1,0:T(8,128)(2,1)} %param.11), channel_id=1, replica_groups=mesh['outer'=2,'row'=16] {'row'}, dimensions={1}, use_global_device_ids=true | all-gather | bytes 974848 | tf_op jit(solution)/shard_map/all_gather | solution.py:30
  47.9 35.3 %all_gather.7 = bf16[32,14336]{1,0:T(8,128)(2,1)S(1)} all-gather(bf16[32,896]{1,0:T(8,128)(2,1)} %param.12), channel_id=1, replica_groups=mesh['outer'=2,'row'=16] {'row'}, dimensions={1}, use_global_device_ids=true | all-gather | bytes 974848 | tf_op jit(solution)/shard_map/all_gather | solution.py:31
  83.1 0.0 copy-start
  83.1 10.4 %fusion.8 = f32[512,32]{0,1:T(8,128)} fusion(bf16[32,14336]{1,0:T(8,128)(2,1)S(1)} %all_gather.6, bf16[1,512,14336]{2,1,0:T(8,128)(2,1)} %param.9), kind=kOutput, calls=%fused_computation.10 | convolution fusion | flops 469762048 | bytes 15663104 | tf_op jit(solution)/shard_map/dot_general | solution.py:12
  93.6 0.0 copy-done
  93.6 5.1 %fusion.4 = f32[512,32]{0,1:T(8,128)} fusion(bf16[32,14336]{1,0:T(8,128)(2,1)S(1)} %all_gather.7, bf16[1,512,14336]{2,1,0:T(8,128)(2,1)S(1)} %copy-done), kind=kOutput, calls=%fused_computation.6 | convolution fusion | flops 469762048 | bytes 15663104 | tf_op jit(solution)/shard_map/dot_general | solution.py:12
  98.7 0.0 all-reduce.8.cloned.1.call-update
  98.7 0.2 all-reduce.6.cloned.1.call-start
  98.9 29.1 %all-reduce.8.cloned.1.call-done = (f32[512,32]{0,1:T(8,128)}, f32[512,32]{0,1:T(8,128)}) async-done(((f32[512,32]{0,1:T(8,128)}, f32[512,32]{0,1:T(8,128)}), (f32[512,32]{0,1:T(8,128)}, f32[512,32]{0,1:T(8,128)})) %all-reduce.8.cloned.1.call-update) | async-done | bytes 131088 | tf_op jit(solution)/shard_map/psum | solution.py:28
  128.0 0.0 copy-start.3
  128.0 9.1 %fusion.2 = f32[32,14336]{1,0:T(8,128)} fusion(bf16[1,512,14336]{2,1,0:T(8,128)(2,1)} %param.10, f32[512,32]{0,1:T(8,128)} %get-tuple-element.14), kind=kOutput, calls=%fused_computation.4 | convolution fusion | flops 469794816 | bytes 16580608 | tf_op jit(solution)/shard_map/dot_general | solution.py:18
  137.1 0.0 copy-done.3
  137.1 9.0 %fusion.6 = f32[32,14336]{1,0:T(8,128)} fusion(bf16[1,512,14336]{2,1,0:T(8,128)(2,1)} %param.9, f32[512,32]{0,1:T(8,128)S(1)} %copy-done.3), kind=kOutput, calls=%fused_computation.8 | convolution fusion | flops 469794816 | bytes 16580608 | tf_op jit(solution)/shard_map/dot_general | solution.py:18
  146.1 0.0 copy-start.2
  146.1 0.0 all-reduce.6.cloned.1.call-update
  146.2 0.1 fusion.32
  146.3 0.7 copy-done.2
  147.0 0.1 fusion.33
  147.1 64.6 %all-reduce.1 = (f32[32,32]{0,1:T(8,128)S(1)}, f32[32,32]{0,1:T(8,128)S(1)}) all-reduce(f32[32,32]{0,1:T(8,128)S(1)} %fusion.32, f32[32,32]{0,1:T(8,128)S(1)} %fusion.33), channel_id=1, replica_groups=mesh['outer'=2,'row'=16] {'row'}, use_global_device_ids=true, to_apply=%region_1.0 | all-reduce | flops 2048 | bytes 16384 | tf_op jit(solution)/shard_map/psum | solution.py:37
  211.7 0.1 copy.11
  211.7 0.1 copy.13
  211.8 2.9 cholesky.55
  214.8 0.6 compare_reduce_fusion
  215.4 0.7 fusion.23
  216.1 2.4 custom-call.11
  218.5 2.9 cholesky.44
  221.5 0.6 compare_reduce_fusion.1
  222.1 0.7 fusion.22
  222.8 2.4 custom-call.10
  225.2 0.3 fusion.18
  225.5 0.0 copy-start.4
  225.5 0.3 fusion.16
  225.8 0.0 copy-start.5
  225.8 60.4 %all-reduce.6.cloned.1.call-done = (f32[32,14336]{1,0:T(8,128)}, f32[32,14336]{1,0:T(8,128)}) async-done(((f32[32,14336]{1,0:T(8,128)}, f32[32,14336]{1,0:T(8,128)}), (f32[32,14336]{1,0:T(8,128)}, f32[32,14336]{1,0:T(8,128)})) %all-reduce.6.cloned.1.call-update) | async-done | bytes 3670032 | tf_op jit(solution)/shard_map/psum | solution.py:45
  286.2 0.0 copy-start.1
  286.2 3.3 fusion.12
  289.5 0.0 copy-done.1
  289.5 0.0 slice-start
  289.5 1.6 fusion.10
  291.1 0.7 constant_dynamic-slice_fusion.1
  291.8 0.7 constant_dynamic-slice_fusion
  292.5 0.0 copy-done.5
  292.5 0.0 slice-start.1
  292.5 0.0 slice-start.2
  292.5 0.0 slice-start.3
  292.5 28.1 %fusion.1 = bf16[1,512,14336]{2,1,0:T(8,128)(2,1)} fusion(f32[32,512]{1,0:T(8,128)S(1)} %fusion.16, f32[32,14336]{1,0:T(8,128)S(1)} %fusion.10, bf16[1,512,14336]{2,1,0:T(8,128)(2,1)} %param.10), kind=kOutput, calls=%fused_computation.3 | convolution fusion | flops 2840592384 | bytes 31260672 | tf_op jit(solution)/shard_map/dot_general | solution.py:55
  320.6 0.0 copy-done.4
  320.6 0.0 slice-done
  320.6 0.0 slice-done.1
  320.6 0.0 slice-done.2
  320.6 0.0 slice-done.3
  320.6 26.7 %fusion = bf16[1,512,14336]{2,1,0:T(8,128)(2,1)} fusion(f32[32,512]{1,0:T(8,128)S(1)} %fusion.18, f32[32,14336]{1,0:T(8,128)S(1)} %fusion.12, bf16[1,512,14336]{2,1,0:T(8,128)(2,1)S(1)} %bitcast.57), kind=kOutput, calls=%fused_computation.2 | convolution fusion | flops 2840592384 | bytes 31260672 | tf_op jit(solution)/shard_map/dot_general | solution.py:53
  (4 shorter events, 0.1 us)
Async XLA Ops:
  7.2 120.8 %all-reduce.8.cloned.1.call-start = ((), (), s32[]{:S(2)}) async-start(), calls=%async_computation.1 | async-start | bytes 262144 | tf_op jit(solution)/shard_map/psum | solution.py:28
  83.1 10.4 %copy-start = (bf16[1,512,14336]{2,1,0:T(8,128)(2,1)S(1)}, bf16[1,512,14336]{2,1,0:T(8,128)(2,1)}, u32[]{:S(2)}) copy-start(bf16[1,512,14336]{2,1,0:T(8,128)(2,1)} %param.10) | copy-start | bytes 44040196
  98.7 187.5 %all-reduce.6.cloned.1.call-start = ((), (), s32[]{:S(2)}) async-start(), calls=%async_computation | async-start | bytes 7340032 | tf_op jit(solution)/shard_map/psum | solution.py:45
  128.0 9.1 %copy-start.3 = (f32[512,32]{0,1:T(8,128)S(1)}, f32[512,32]{0,1:T(8,128)}, u32[]{:S(2)}) copy-start(f32[512,32]{0,1:T(8,128)} %get-tuple-element.13) | copy-start | bytes 196612
  146.1 0.8 copy-start.2
  225.5 95.1 %copy-start.4 = (f32[32,512]{1,0:T(8,128)}, f32[32,512]{1,0:T(8,128)S(1)}, u32[]{:S(2)}) copy-start(f32[32,512]{1,0:T(8,128)S(1)} %fusion.18) | copy-start | bytes 196612
  225.8 66.7 %copy-start.5 = (f32[32,512]{1,0:T(8,128)}, f32[32,512]{1,0:T(8,128)S(1)}, u32[]{:S(2)}) copy-start(f32[32,512]{1,0:T(8,128)S(1)} %fusion.16) | copy-start | bytes 196612
  286.2 3.3 copy-start.1
  289.5 31.1 %slice-start = ((s8[14680064]{0:T(1024)(128)(4,1)}), s8[4194304]{0:T(1024)(128)(4,1)S(1)}, s32[]{:S(2)}) async-start(s8[14680064]{0:T(1024)(128)(4,1)} %bitcast.56), calls=%async_computation.2 | async-start | bytes 8388608
  292.5 28.1 %slice-start.1 = ((s8[14680064]{0:T(1024)(128)(4,1)}), s8[4194304]{0:T(1024)(128)(4,1)S(1)}, s32[]{:S(2)}) async-start(s8[14680064]{0:T(1024)(128)(4,1)} %bitcast.56), calls=%async_computation.3 | async-start | bytes 8388608
  292.5 28.1 %slice-start.2 = ((s8[14680064]{0:T(1024)(128)(4,1)}), s8[4194304]{0:T(1024)(128)(4,1)S(1)}, s32[]{:S(2)}) async-start(s8[14680064]{0:T(1024)(128)(4,1)} %bitcast.56), calls=%async_computation.4 | async-start | bytes 8388608
  292.5 28.1 %slice-start.3 = ((s8[14680064]{0:T(1024)(128)(4,1)}), s8[2097152]{0:T(1024)(128)(4,1)S(1)}, s32[]{:S(2)}) async-start(s8[14680064]{0:T(1024)(128)(4,1)} %bitcast.56), calls=%async_computation.5 | async-start | bytes 4194304
Sparse Core Ops, SparseCore 0:
  98.8 29.1 all-reduce.7
  146.3 139.8 all-reduce.5
where the time goes:
time: 357 us; the launch traced here: 354 us
  blocking collectives  140 us (39%)
  matrix products  94.2 us (26%)
  waiting for transfers between devices  89.5 us (25%)
  between operations  14.2 us (4%)
  other arithmetic  13.4 us (4%)
    psum x1, blocking collectives, local(): lax.psum((contract_rows(round_gate, round_gate), contract_rows(round_up,...  64.6 us
    psum x1, waiting for transfers between devices, local(): totals = lax.psum((products[0], products[1]), ('outer', 'row'))  60.4 us
    all_gather x1, blocking collectives, local(): lax.all_gather(basis_gate, 'row', axis=1, tiled=True)  40.6 us
    all_gather x1, blocking collectives, local(): lax.all_gather(basis_up, 'row', axis=1, tiled=True)  35.3 us
    psum x1, waiting for transfers between devices, local(): lax.psum((contract_cols(gate_rows, lax.all_gather(basis_gate, 'row', axis...  29.1 us
    dot_general x1, matrix products, local(): jnp.dot(factor_up, full_up, precision=lax.Precision.HIGHEST)  28.1 us
    dot_general x1, matrix products, local(): jnp.dot(factor_gate, full_gate, precision=lax.Precision.HIGHEST)  26.7 us
    dot_general x4, matrix products, contract_rows(): lax.dot_general(left, right, (((0,), (0,)), ((), ())), preferred_element_...  18.4 us
  transfers between devices with their start and end apart: 2, of which 2 were waited for; matrix products, arithmetic and copies ran while one was open for 4% of the time, Pallas kernels for 0%

commit v1 on v0

--- a/solution.py
+++ b/solution.py
@@ -1,7 +1,14 @@
+import functools
+
 import jax
 import jax.numpy as jnp
 from jax import lax
+from jax.experimental import pallas as pl
+from jax.experimental.pallas import tpu as pltpu
 from jax.sharding import PartitionSpec as P
+
+MESH = pl.DeviceIdType.MESH
+HIGHEST = lax.Precision.HIGHEST
 
 
 def forward_solve(lower_matrix, right_hand):
@@ -58,9 +65,430 @@
     return (next_gate, next_up, factor_gate, factor_up, resid_gate[None], resid_up[None])
 
 
+def gather_kernel(
+    n, pods, g0_ref, g1_ref, b0_ref, b1_ref,
+    s0_ref, s1_ref, prt_ref, linv_ref, own_ref,
+    grads, basis, sfull, acc, csend, crecv, rsend, rrecv, pacc, ptsend, ptrecv,
+    gsend, grecv, own, send_sems, recv_sems, g_sems, out_sems,
+):
+    m = n.bit_length() - 1
+    Q = n // 4
+    me = lax.axis_index("row")
+    core = lax.axis_index("outer")
+    rank = prt_ref.shape[1]
+    half = rank // 2
+    cols = b0_ref.shape[1]
+    grad_refs = (g0_ref, g1_ref)
+    basis_refs = (b0_ref, b1_ref)
+    out_refs = (s0_ref, s1_ref)
+
+    delta = [(1 - 2 * ((me // 2**b) % 2)) * 2**b for b in range(m)]
+    slot_delta = [delta[m - 1 - i] for i in range(m - 2)] + [delta[0], delta[1]]
+
+    def block_of(q):
+        place = me
+        for i in range(m):
+            place = place + ((q // 2**i) % 2) * slot_delta[i]
+        return place
+
+    near = {"row": me + (1 - core) * delta[0] + core * delta[1]}
+    far = {"row": me + (1 - core) * delta[1] + core * delta[0]}
+    partner = [{"row": me + delta[m - 1 - i]} for i in range(m - 2)]
+    twin = {"outer": 1 - core}
+
+    used = [0]
+    sent = []
+
+    def push(src, dst, target):
+        i = used[0]
+        used[0] += 1
+        copy = pltpu.make_async_remote_copy(
+            src_ref=src, dst_ref=dst, send_sem=send_sems.at[i], recv_sem=recv_sems.at[i],
+            device_id=target, device_id_type=MESH,
+        )
+        copy.start()
+        sent.append(copy)
+        return copy
+
+    def load(mat, q):
+        start = pl.multiple_of(block_of(q) * cols, 128)
+        return pltpu.make_async_copy(
+            grad_refs[mat].at[0, :, pl.ds(start, cols)], grads.at[mat, q],
+            g_sems.at[mat * n + q],
+        )
+
+    def load_all(mat):
+        @pl.loop(0, n)
+        def _(q):
+            load(mat, q).start()
+
+    barrier = pltpu.get_barrier_semaphore()
+    greeted = partner + [{"row": me + delta[0]}, {"row": me + delta[1]}, twin]
+    for target in greeted:
+        pl.semaphore_signal(barrier, inc=1, device_id=target, device_id_type=MESH)
+    load_all(0)
+    load_all(1)
+    for mat in range(2):
+        basis[mat, 0] = basis_refs[mat][...].reshape(2, half, cols)
+        pacc[mat] = jnp.zeros(pacc.shape[1:], jnp.float32)
+    pl.semaphore_wait(barrier, len(greeted))
+
+    class Gather:
+        def __init__(self, ref):
+            self.ref = ref
+            self.moves = {}
+            self.swaps = {}
+
+        def go(self, name, src, dst, size, target):
+            self.moves[name] = (
+                push(
+                    self.ref.at[pl.ds(src, size), core], self.ref.at[pl.ds(dst, size), core], target
+                ),
+                dst,
+                size,
+            )
+
+        def start(self, i):
+            if i < m - 2:
+                self.go(i, 0, 2**i, 2**i, partner[i])
+            elif i == m - 2:
+                self.go("near", 0, (1 + core) * Q, Q, near)
+                self.go("far", 0, (2 - core) * Q, Q, far)
+            else:
+                self.go("last", (1 + core) * Q, 3 * Q, Q, far)
+
+        def land(self, name):
+            copy, dst, size = self.moves[name]
+            copy.wait_recv()
+            region = self.ref.at[pl.ds(dst, size), core]
+            self.swaps[name] = push(region, region, twin)
+
+        def swapped(self, name):
+            self.swaps[name].wait_recv()
+
+        def step(self, i):
+            if i < m - 2:
+                self.land(i)
+                self.start(i + 1)
+            elif i == m - 2:
+                self.land("near")
+                self.start(i + 1)
+                self.land("far")
+            else:
+                self.land("last")
+
+    def project(mat, base, size):
+        @pl.loop(0, size)
+        def _(k):
+            q = base + k
+            load(mat, q).wait()
+            pacc[mat] += contract_cols(grads[mat, q], basis[mat, q].reshape(rank, cols))
+
+    gathers = [Gather(basis.at[mat]) for mat in range(2)]
+    for mat in range(2):
+        gathers[mat].start(0)
+    for mat in range(2):
+        project(mat, 0, 1)
+    for i in range(m):
+        for mat in range(2):
+            gathers[mat].step(i)
+        if 1 <= i <= m - 2:
+            for mat in range(2):
+                gathers[mat].swapped(i - 1)
+                project(mat, 2 ** (i - 1), 2 ** (i - 1))
+    pt_copy = []
+    for mat in range(2):
+        for name in ("near", "far", "last"):
+            gathers[mat].swapped(name)
+        project(mat, Q, 3 * Q)
+        ptsend[mat] = pacc[mat].T
+        pt_copy.append(push(ptsend.at[mat], ptrecv.at[mat], twin))
+
+    grams = [[], []]
+
+    def round_product(mat):
+        pt_copy[mat].wait_recv()
+        prt_ref[mat] = ((ptsend[mat] + ptrecv[mat]) / pods).astype(jnp.bfloat16)
+        gsend[mat, 0] = contract_cols(prt_ref[mat], prt_ref[mat])
+
+    def gram_tasks():
+        for k in range(m):
+            target = {"row": me + delta[m - 1 - k]}
+            copies = [push(gsend.at[mat, k], grecv.at[mat, k], target) for mat in range(2)]
+            yield
+            for mat in range(2):
+                copies[mat].wait_recv()
+                gsend[mat, k + 1] = gsend[mat, k] + grecv[mat, k]
+        sub = lax.broadcasted_iota(jnp.int32, (rank, 2 * rank), 0)
+        lane = lax.broadcasted_iota(jnp.int32, (rank, 2 * rank), 1)
+        unit = jnp.where(lane == sub + rank, 1.0, 0.0).astype(jnp.float32)[:, rank:]
+        systems = [jnp.concatenate([gsend[mat, m], unit], axis=1) for mat in range(2)]
+        for k in range(rank):
+            for mat in range(2):
+                system = systems[mat]
+                scale = 1.0 / jnp.sqrt(system[k : k + 1, k : k + 1])
+                row = system[k : k + 1, :] * scale
+                column = system[:, k : k + 1] * scale
+                systems[mat] = jnp.where(
+                    sub == k, row, jnp.where(sub > k, system - column * row, system)
+                )
+            if k % 8 == 7 and k < rank - 1:
+                yield
+        for mat in range(2):
+            linv_ref[mat] = systems[mat][:, rank:]
+
+    core_copy = [{}, {}]
+    moved = [{}, {}]
+
+    def multiply(mat, group):
+        @pl.loop(group * Q, (group + 1) * Q)
+        def _(q):
+            product = jnp.dot(
+                prt_ref[mat], grads[mat, q], preferred_element_type=jnp.float32
+            )
+            low, high = product[:half], product[half:]
+            acc[mat, q] = jnp.where(core == 0, low, high)
+            csend[mat, q] = jnp.where(core == 0, high, low).astype(jnp.bfloat16)
+
+        region = pl.ds(group * Q, Q)
+        core_copy[mat][group] = push(csend.at[mat, region], crecv.at[mat, region], twin)
+
+    def add_core(mat, group):
+        core_copy[mat][group].wait_recv()
+        region = pl.ds(group * Q, Q)
+        acc[mat, region] += crecv[mat, region].astype(jnp.float32)
+
+    def reduce_send(mat, name, base, size, place, target):
+        spot = pl.ds(place, size)
+        rsend[mat, spot] = acc[mat, pl.ds(base, size)].astype(jnp.bfloat16)
+        moved[mat][name] = (
+            push(rsend.at[mat, spot], rrecv.at[mat, spot], target), place, size,
+        )
+
+    def reduce_add(mat, name, base):
+        copy, place, size = moved[mat][name]
+        copy.wait_recv()
+        acc[mat, pl.ds(base, size)] += rrecv[mat, pl.ds(place, size)].astype(jnp.float32)
+
+    def product_tasks(mat):
+        multiply(mat, 3)
+        yield
+        multiply(mat, 2)
+        yield
+        add_core(mat, 3)
+        reduce_send(mat, "second", 3 * Q, Q, Q, far)
+        multiply(mat, 1)
+        yield
+        multiply(mat, 0)
+        add_core(mat, 2)
+        add_core(mat, 1)
+        reduce_send(mat, "first", (2 - core) * Q, Q, 0, far)
+        yield
+
+    def reduce_tasks(mat):
+        reduce_add(mat, "second", (1 + core) * Q)
+        reduce_send(mat, "near", (1 + core) * Q, Q, 2 * Q, near)
+        yield
+        add_core(mat, 0)
+        reduce_add(mat, "first", 0)
+        yield
+        reduce_add(mat, "near", 0)
+        for i in reversed(range(m - 2)):
+            reduce_send(mat, i, 2**i, 2**i, 3 * Q + Q - 2 ** (i + 1), partner[i])
+            yield
+            reduce_add(mat, i, 0)
+        mine = acc[mat, 0] / pods
+        own[mat, core] = mine
+        sfull[mat, 0, core] = mine.astype(jnp.bfloat16)
+        gather = Gather(sfull.at[mat])
+        gather.start(0)
+        own_copy = push(own.at[mat, core], own.at[mat, core], twin)
+        region = sfull.at[mat, pl.ds(0, 1), core]
+        gather.swaps["own"] = push(region, region, twin)
+        yield
+        for i in range(m):
+            gather.step(i)
+            yield
+        own_copy.wait_recv()
+        own_ref[mat] = own[mat].reshape(rank, cols)
+        for name in gather.swaps:
+            gather.swapped(name)
+
+        for q in range(n):
+            pltpu.make_async_copy(
+                sfull.at[mat, q], out_refs[mat].at[block_of(q)], out_sems.at[mat * n + q]
+            ).start()
+        yield
+
+    def drive(tasks, first_only=False):
+        live = list(tasks)
+        while live:
+            for task in list(live):
+                if next(task, StopIteration) is StopIteration:
+                    live.remove(task)
+                    if first_only and task is tasks[0]:
+                        return
+
+    round_product(0)
+    gate_product = product_tasks(0)
+    next(gate_product)
+    next(gate_product)
+    round_product(1)
+    gram = gram_tasks()
+    next(gram)
+    drive([gate_product])
+    gate_reduce = reduce_tasks(0)
+    up_reduce = reduce_tasks(1)
+    drive([product_tasks(1), gate_reduce, gram], first_only=True)
+    drive([gate_reduce, up_reduce, gram])
+    for mat in range(2):
+        for q in range(n):
+            pltpu.make_async_copy(
+                sfull.at[mat, q], out_refs[mat].at[block_of(q)], out_sems.at[mat * n + q]
+            ).wait()
+    for copy in sent:
+        copy.wait_send()
+
+
+def copies_of(n):
+    m = n.bit_length() - 1
+    gather = 2 * (m + 1)
+    return 2 * (gather + 1 + m + 4 + (m + 1) + gather + 2)
+
+
+def residual_kernel(
+    g0_ref, g1_ref, s0_ref, s1_ref, prt_ref, linv_ref, own_ref,
+    next0_ref, next1_ref, factor0_ref, factor1_ref, r0_ref, r1_ref, left,
+):
+    @pl.when(pl.program_id(0) == 0)
+    def _():
+        for mat, (next_ref, factor_ref) in enumerate(
+            ((next0_ref, factor0_ref), (next1_ref, factor1_ref))
+        ):
+            inverse = linv_ref[mat]
+            next_ref[...] = jnp.dot(inverse, own_ref[mat], precision=HIGHEST)
+            columns = jnp.dot(inverse, prt_ref[mat].astype(jnp.float32), precision=HIGHEST)
+            factor = columns.T
+            factor_ref[...] = factor
+            mixed = jnp.dot(factor, inverse, precision=HIGHEST)
+            top = mixed.astype(jnp.bfloat16)
+            rest = (mixed - top.astype(jnp.float32)).astype(jnp.bfloat16)
+            left[mat] = jnp.concatenate([top, rest], axis=1)
+
+    for mat, (g_ref, s_ref, r_ref) in enumerate(
+        ((g0_ref, s0_ref, r0_ref), (g1_ref, s1_ref, r1_ref))
+    ):
+        rank = prt_ref.shape[1]
+        block = s_ref[0].reshape(rank, s_ref.shape[3])
+        both = jnp.concatenate([block, block], axis=0)
+        product = jnp.dot(left[mat], both, preferred_element_type=jnp.float32)
+        r_ref[0] = (g_ref[0].astype(jnp.float32) - product).astype(jnp.bfloat16)
+
+
+def fused(n, pods, grad_gate, grad_up, basis_gate, basis_up):
+    _, rows, full_cols = grad_gate.shape
+    rank, cols = basis_gate.shape
+    half = rank // 2
+    m = n.bit_length() - 1
+    vmem = pl.BlockSpec(memory_space=pltpu.VMEM)
+    anywhere = pl.BlockSpec(memory_space=pl.ANY)
+    f32, bf16 = jnp.float32, jnp.bfloat16
+    count = copies_of(n)
+    s_gate, s_up, prt, linv, own = pl.pallas_call(
+        functools.partial(gather_kernel, n, pods),
+        out_shape=[
+            jax.ShapeDtypeStruct((n, 2, half, cols), bf16),
+            jax.ShapeDtypeStruct((n, 2, half, cols), bf16),
+            jax.ShapeDtypeStruct((2, rank, rows), bf16),
+            jax.ShapeDtypeStruct((2, rank, rank), f32),
+            jax.ShapeDtypeStruct((2, rank, cols), f32),
+        ],
+        in_specs=[anywhere, anywhere, vmem, vmem],
+        out_specs=[anywhere, anywhere, vmem, vmem, vmem],
+        scratch_shapes=[
+            pltpu.VMEM((2, n, rows, cols), bf16),
+            pltpu.VMEM((2, n, 2, half, cols), bf16),
+            pltpu.VMEM((2, n, 2, half, cols), bf16),
+            pltpu.VMEM((2, n, half, cols), f32),
+            pltpu.VMEM((2, n, half, cols), bf16),
+            pltpu.VMEM((2, n, half, cols), bf16),
+            pltpu.VMEM((2, n, half, cols), bf16),
+            pltpu.VMEM((2, n, half, cols), bf16),
+            pltpu.VMEM((2, rows, rank), f32),
+            pltpu.VMEM((2, rank, rows), f32),
+            pltpu.VMEM((2, rank, rows), f32),
+            pltpu.VMEM((2, m + 1, rank, rank), f32),
+            pltpu.VMEM((2, m, rank, rank), f32),
+            pltpu.VMEM((2, 2, half, cols), f32),
+            pltpu.SemaphoreType.DMA((count,)),
+            pltpu.SemaphoreType.DMA((count,)),
+            pltpu.SemaphoreType.DMA((2 * n,)),
+            pltpu.SemaphoreType.DMA((2 * n,)),
+        ],
+        compiler_params=pltpu.CompilerParams(
+            collective_id=0, has_side_effects=True, vmem_limit_bytes=56 * 2**20
+        ),
+        cost_estimate=pl.CostEstimate(
+            flops=8 * rows * full_cols * rank,
+            bytes_accessed=4 * rows * full_cols,
+            transcendentals=0,
+        ),
+    )(grad_gate, grad_up, basis_gate, basis_up)
+
+    def whole(array):
+        return pl.BlockSpec(array.shape, lambda i: (0,) * array.ndim)
+
+    def fixed(*shape):
+        return pl.BlockSpec(shape, lambda i: (0,) * len(shape))
+
+    block = pl.BlockSpec((1, rows, cols), lambda i: (0, 0, i))
+    right = pl.BlockSpec((1, 2, half, cols), lambda i: (i, 0, 0, 0))
+    return tuple(
+        pl.pallas_call(
+            residual_kernel,
+            grid=(n,),
+            out_shape=[
+                jax.ShapeDtypeStruct((rank, cols), f32),
+                jax.ShapeDtypeStruct((rank, cols), f32),
+                jax.ShapeDtypeStruct((rows, rank), f32),
+                jax.ShapeDtypeStruct((rows, rank), f32),
+                jax.ShapeDtypeStruct(grad_gate.shape, bf16),
+                jax.ShapeDtypeStruct(grad_up.shape, bf16),
+            ],
+            in_specs=[block, block, right, right, whole(prt), whole(linv), whole(own)],
+            out_specs=[
+                fixed(rank, cols), fixed(rank, cols), fixed(rows, rank), fixed(rows, rank),
+                block, block,
+            ],
+            scratch_shapes=[pltpu.VMEM((2, rows, 2 * rank), bf16)],
+            compiler_params=pltpu.CompilerParams(vmem_limit_bytes=48 * 2**20),
+            cost_estimate=pl.CostEstimate(
+                flops=4 * rows * full_cols * rank,
+                bytes_accessed=8 * rows * full_cols,
+                transcendentals=0,
+            ),
+        )(grad_gate, grad_up, s_gate, s_up, prt, linv, own)
+    )
+
+
+def dispatch(grad_gate, grad_up, basis_gate, basis_up):
+    n = lax.axis_size("row")
+    pods = lax.axis_size("outer")
+    pod_part, rows, full_cols = grad_gate.shape
+    rank, cols = basis_gate.shape
+    fits = (
+        pods == 2 and pod_part == 1 and n >= 4 and n & (n - 1) == 0
+        and cols % 128 == 0 and rows % 128 == 0 and rank % 32 == 0
+        and 4 * rows * full_cols <= 36 * 2**20
+    )
+    if fits:
+        return fused(n, pods, grad_gate, grad_up, basis_gate, basis_up)
+    return local(grad_gate, grad_up, basis_gate, basis_up)
+
+
 def solution(mesh):
     return jax.shard_map(
-        local,
+        dispatch,
         mesh=mesh,
         in_specs=(P("outer", "row", None), P("outer", "row", None), P(None, "row"), P(None, "row")),
         out_specs=(

time: 357 us -> 120 us (0.34)
  blocking collectives: 140 us -> 0 us
  Pallas kernels: 0 us -> 112 us
  matrix products: 94.2 us -> 0 us
  waiting for transfers between devices: 89.5 us -> 0 us
  between operations: 14.2 us -> 0.65 us
  other arithmetic: 13.4 us -> 0 us
  local copies, waits for them, and re-layouts: 2.19 us -> 6.36 us
    pallas_call x0 -> x2, Pallas kernels: none -> 112 us  [the longest x1 84.4 us: fused(): pl.pallas_call(functools.partial(gather_kernel, n, pods), out_shape=[jax....]
    psum x2 -> x0, waiting for transfers between devices: 89.4 us -> none  [the longest x1 60.4 us: local(): totals = lax.psum((products[0], products[1]), ('outer', 'row'))]
    dot_general x8 -> x0, matrix products: 88.8 us -> none  [the longest x1 28.1 us: local(): jnp.dot(factor_up, full_up, precision=lax.Precision.HIGHEST)]
    all_gather x2 -> x0, blocking collectives: 75.9 us -> none  [the longest x1 40.6 us: local(): lax.all_gather(basis_gate, 'row', axis=1, tiled=True)]
    psum x1 -> x0, blocking collectives: 64.6 us -> none  [local(): lax.psum((contract_rows(round_gate, round_gate), contract_rows(round_up,...]
    another operation x10 -> x0, other arithmetic: 13.4 us -> none  [the longest x4 6.17 us: forward_solve(): jax.scipy.linalg.solve_triangular(lower_matrix, right_hand, lower=True)]
    another operation x4 -> x0, matrix products: 5.45 us -> none  [forward_solve(): jax.scipy.linalg.solve_triangular(lower_matrix, right_hand, lower=True)]
    unnamed x20 -> x10, local copies, waits for them, and re-layouts: 0.73 us -> 4.88 us
  transfers between devices with their start and end apart: 2 -> 0, of which waited for: 2 -> 0; matrix products, arithmetic and copies ran while one was open for 4% -> 0% of each run, Pallas kernels for 0% -> 0%
where the time goes in v1:
time: 120 us; the launch traced here: 119 us
  Pallas kernels  112 us (93%)
  local copies, waits for them, and re-layouts  6.36 us (5%)
    pallas_call x1, Pallas kernels, fused(): pl.pallas_call(functools.partial(gather_kernel, n, pods), out_shape=[jax....  84.4 us
    pallas_call x1, Pallas kernels, fused(): pl.pallas_call(residual_kernel, grid=(n,), out_shape=[jax.ShapeDtypeStruc...  27.2 us
    unnamed x10, local copies, waits for them, and re-layouts  4.88 us

profile of v1, /device:TPU:1, one launch (start us, length us, event | category | flops | bytes accessed | tf_op | source)
XLA Modules:
  0.0 118.7 jit_solution(9737811686160616075)
XLA Ops:
  0.6 84.4 %shard_map.91 = (bf16[16,2,16,896]{3,2,1,0:T(8,128)(2,1)}, bf16[16,2,16,896]{3,2,1,0:T(8,128)(2,1)}, bf16[2,32,512]{2,1,0:T(8,128)(2,1)}, f32[2,32,32]{2,1,0:T(8,128)}, f32[2,32,896]{2,1,0:T(8,128)}) custom-call(bf16[1,512,14336]{2,1,0:T(8,128)(2,1)} %g0_ref.3, bf16[1,512,14336]{2,1,0:T(8,128)(2,1)} %g1_ref.3, bf16[32,896]{1,0:T(8,128)(2,1)} %b0_ref.1, ...), custom_call_target="tpu_custom_call" | custom-call | flops 1879048192 | bytes 29360128 | tf_op jit(solution)/shard_map/pallas_call | solution.py:397
  85.1 0.0 copy-start
  85.1 1.2 copy-done
  86.3 0.0 copy-start.1
  86.3 1.2 copy-done.1
  87.4 0.0 copy-start.2
  87.4 0.9 copy-done.2
  88.4 0.0 copy-start.3
  88.4 0.8 copy-done.3
  89.2 0.0 copy-start.4
  89.2 0.8 copy-done.4
  90.0 27.2 %shard_map.92 = (f32[32,896]{1,0:T(8,128)}, f32[32,896]{1,0:T(8,128)}, f32[512,32]{1,0:T(8,128)S(1)}, f32[512,32]{1,0:T(8,128)S(1)}, bf16[1,512,14336]{2,1,0:T(8,128)(2,1)}, /*index=5*/bf16[1,512,14336]{2,1,0:T(8,128)(2,1)}) custom-call(bf16[1,512,14336]{2,1,0:T(8,128)(2,1)} %g0_ref.3, bf16[1,512,14336]{2,1,0:T(8,128)(2,1)} %g1_ref.3, ...), custom_call_target="tpu_custom_call" | custom-call | flops 939524096 | bytes 58720256 | tf_op jit(solution)/shard_map/pallas_call | solution.py:447
  117.2 0.7 copy.10
  118.0 0.7 copy.11
Async XLA Ops:
  85.1 1.2 copy-start
  86.3 1.2 copy-start.1
  87.4 0.9 copy-start.2
  88.4 0.8 copy-start.3
  89.2 0.8 copy-start.4

commit v2 on v0

--- a/solution.py
+++ b/solution.py
@@ -1,7 +1,14 @@
+import functools
+
 import jax
 import jax.numpy as jnp
 from jax import lax
+from jax.experimental import pallas as pl
+from jax.experimental.pallas import tpu as pltpu
 from jax.sharding import PartitionSpec as P
+
+MESH = pl.DeviceIdType.MESH
+HIGHEST = lax.Precision.HIGHEST
 
 
 def forward_solve(lower_matrix, right_hand):
@@ -58,9 +65,488 @@
     return (next_gate, next_up, factor_gate, factor_up, resid_gate[None], resid_up[None])
 
 
+class Place:
+    def __init__(self, n, send_sems, recv_sems):
+        self.m = n.bit_length() - 1
+        self.Q = n // 4
+        self.me = lax.axis_index("row")
+        self.core = lax.axis_index("outer")
+        m = self.m
+        delta = [(1 - 2 * ((self.me // 2**b) % 2)) * 2**b for b in range(m)]
+        self.delta = delta
+        self.slot_delta = [delta[m - 1 - i] for i in range(m - 2)] + [delta[0], delta[1]]
+        self.near = {"row": self.me + (1 - self.core) * delta[0] + self.core * delta[1]}
+        self.far = {"row": self.me + (1 - self.core) * delta[1] + self.core * delta[0]}
+        self.partner = [{"row": self.me + delta[m - 1 - i]} for i in range(m - 2)]
+        self.twin = {"outer": 1 - self.core}
+        self.sems = (send_sems, recv_sems)
+        self.sent = []
+
+    def block_of(self, q):
+        place = self.me
+        for i in range(self.m):
+            place = place + ((q // 2**i) % 2) * self.slot_delta[i]
+        return place
+
+    def greet(self):
+        barrier = pltpu.get_barrier_semaphore()
+        targets = self.partner + [
+            {"row": self.me + self.delta[0]}, {"row": self.me + self.delta[1]}, self.twin,
+        ]
+        for target in targets:
+            pl.semaphore_signal(barrier, inc=1, device_id=target, device_id_type=MESH)
+        return lambda: pl.semaphore_wait(barrier, len(targets))
+
+    def push(self, src, dst, target):
+        i = len(self.sent)
+        copy = pltpu.make_async_remote_copy(
+            src_ref=src, dst_ref=dst, send_sem=self.sems[0].at[i], recv_sem=self.sems[1].at[i],
+            device_id=target, device_id_type=MESH,
+        )
+        copy.start()
+        self.sent.append(copy)
+        return copy
+
+
+class Gather:
+    def __init__(self, place, ref):
+        self.at = place
+        self.ref = ref
+        self.moves = {}
+        self.swaps = {}
+
+    def go(self, name, src, dst, size, target):
+        core = self.at.core
+        copy = self.at.push(
+            self.ref.at[pl.ds(src, size), core], self.ref.at[pl.ds(dst, size), core], target
+        )
+        self.moves[name] = (copy, dst, size)
+
+    def start(self, i):
+        m, Q, core = self.at.m, self.at.Q, self.at.core
+        if i < m - 2:
+            self.go(i, 0, 2**i, 2**i, self.at.partner[i])
+        elif i == m - 2:
+            self.go("near", 0, (1 + core) * Q, Q, self.at.near)
+            self.go("far", 0, (2 - core) * Q, Q, self.at.far)
+        else:
+            self.go("last", (1 + core) * Q, 3 * Q, Q, self.at.far)
+
+    def land(self, name):
+        copy, dst, size = self.moves[name]
+        copy.wait_recv()
+        self.swap(name, dst, size)
+
+    def swap(self, name, dst, size):
+        region = self.ref.at[pl.ds(dst, size), self.at.core]
+        self.swaps[name] = self.at.push(region, region, self.at.twin)
+
+    def swapped(self, name):
+        self.swaps[name].wait_recv()
+
+    def step(self, i):
+        m = self.at.m
+        if i < m - 2:
+            self.land(i)
+            self.start(i + 1)
+        elif i == m - 2:
+            self.land("near")
+            self.start(i + 1)
+            self.land("far")
+        else:
+            self.land("last")
+
+
+def forward_kernel(
+    n, pods, g0_ref, g1_ref, b0_ref, b1_ref, grads,
+    prt_ref, basis, pacc, ptsend, ptrecv, sfull, acc, csend, crecv, rsend, rrecv, gsend, grecv, own,
+    send_sems, recv_sems, g_sems,
+):
+    at = Place(n, send_sems, recv_sems)
+    copies = project_part(
+        at, n, g0_ref, g1_ref, b0_ref, b1_ref, grads, basis, pacc, ptsend, ptrecv, g_sems,
+    )
+
+    def round_product(mat):
+        copies[mat].wait_recv()
+        prt_ref[mat] = ((ptsend[mat] + ptrecv[mat]) / pods).astype(jnp.bfloat16)
+        rows, rank = prt_ref.shape[2], prt_ref.shape[1]
+        grads[mat, rows + rank :, :rows] = prt_ref[mat]
+        gsend[mat, 0] = contract_cols(prt_ref[mat], prt_ref[mat])
+
+    reduce_part(
+        at, n, pods, b0_ref.shape[1], round_product, grads, prt_ref,
+        sfull, acc, csend, crecv, rsend, rrecv, gsend, grecv, own,
+    )
+    for copy in at.sent:
+        copy.wait_send()
+
+
+def pack_of(rank, rows, cols):
+    return rows + rank, rows, rows + 3 * cols
+
+
+def terms(value):
+    top = value.astype(jnp.bfloat16)
+    rest = value - top.astype(jnp.float32)
+    middle = rest.astype(jnp.bfloat16)
+    return top, middle, (rest - middle.astype(jnp.float32)).astype(jnp.bfloat16)
+
+
+def project_part(
+    at, n, g0_ref, g1_ref, b0_ref, b1_ref, grads, basis, pacc, ptsend, ptrecv, g_sems,
+):
+    m, Q = at.m, at.Q
+    rank, cols = b0_ref.shape
+    grad_refs = (g0_ref, g1_ref)
+    basis_refs = (b0_ref, b1_ref)
+
+    def columns(q):
+        return pl.ds(pl.multiple_of(at.block_of(q) * cols, 128), cols)
+
+    def load(mat, q):
+        return pltpu.make_async_copy(
+            grad_refs[mat].at[0, :, columns(q)], grads.at[mat, pl.ds(0, grad_refs[mat].shape[1]), columns(q)],
+            g_sems.at[mat * n + q],
+        )
+
+    greeted = at.greet()
+    for mat in range(2):
+        @pl.loop(0, n)
+        def _(q):
+            load(mat, q).start()
+
+        basis[mat, 0] = basis_refs[mat][...].reshape(2, rank // 2, cols)
+        pacc[mat] = jnp.zeros(pacc.shape[1:], jnp.float32)
+    greeted()
+
+    def project(mat, base, size):
+        @pl.loop(0, size)
+        def _(k):
+            q = base + k
+            load(mat, q).wait()
+            pacc[mat] += contract_cols(
+                grads[mat, pl.ds(0, grad_refs[mat].shape[1]), columns(q)], basis[mat, q].reshape(rank, cols)
+            )
+
+    gathers = [Gather(at, basis.at[mat]) for mat in range(2)]
+    for mat in range(2):
+        gathers[mat].start(0)
+    for mat in range(2):
+        project(mat, 0, 1)
+    for i in range(m):
+        for mat in range(2):
+            gathers[mat].step(i)
+        if 1 <= i <= m - 2:
+            for mat in range(2):
+                gathers[mat].swapped(i - 1)
+                project(mat, 2 ** (i - 1), 2 ** (i - 1))
+    copies = []
+    for mat in range(2):
+        for name in ("near", "far", "last"):
+            gathers[mat].swapped(name)
+        project(mat, Q, 3 * Q)
+        ptsend[mat] = pacc[mat].T
+        copies.append(at.push(ptsend.at[mat], ptrecv.at[mat], at.twin))
+    return copies
+
+
+def reduce_part(
+    at, n, pods, cols, round_product, grads, prt_ref,
+    sfull, acc, csend, crecv, rsend, rrecv, gsend, grecv, own,
+):
+    m, Q, core, near, far = at.m, at.Q, at.core, at.near, at.far
+    rank, rows = prt_ref.shape[1:]
+    half = rank // 2
+    row_spot, own_spot, linv_spot = pack_of(rank, rows, cols)
+
+    def columns(q):
+        return pl.ds(pl.multiple_of(at.block_of(q) * cols, 128), cols)
+
+    def gram_tasks():
+        for k in range(m):
+            target = {"row": at.me + at.delta[m - 1 - k]}
+            copies = [at.push(gsend.at[mat, k], grecv.at[mat, k], target) for mat in range(2)]
+            yield
+            for mat in range(2):
+                copies[mat].wait_recv()
+                gsend[mat, k + 1] = gsend[mat, k] + grecv[mat, k]
+        sub = lax.broadcasted_iota(jnp.int32, (rank, 2 * rank), 0)
+        lane = lax.broadcasted_iota(jnp.int32, (rank, 2 * rank), 1)
+        unit = jnp.where(lane == sub + rank, 1.0, 0.0).astype(jnp.float32)[:, rank:]
+        systems = [jnp.concatenate([gsend[mat, m], unit], axis=1) for mat in range(2)]
+        for k in range(rank):
+            for mat in range(2):
+                system = systems[mat]
+                scale = 1.0 / jnp.sqrt(system[k : k + 1, k : k + 1])
+                row = system[k : k + 1, :] * scale
+                column = system[:, k : k + 1] * scale
+                systems[mat] = jnp.where(
+                    sub == k, row, jnp.where(sub > k, system - column * row, system)
+                )
+            if k % 8 == 7 and k < rank - 1:
+                yield
+        for mat in range(2):
+            for part, value in enumerate(terms(systems[mat][:, rank:])):
+                start = linv_spot + part * 128
+                grads[mat, row_spot:, start : start + rank] = value
+
+    core_copy = [{}, {}]
+    moved = [{}, {}]
+
+    def multiply(mat, group):
+        @pl.loop(group * Q, (group + 1) * Q)
+        def _(q):
+            product = jnp.dot(
+                prt_ref[mat], grads[mat, pl.ds(0, rows), columns(q)], preferred_element_type=jnp.float32
+            )
+            low, high = product[:half], product[half:]
+            acc[mat, q] = jnp.where(core == 0, low, high)
+            csend[mat, q] = jnp.where(core == 0, high, low).astype(jnp.bfloat16)
+
+        region = pl.ds(group * Q, Q)
+        core_copy[mat][group] = at.push(csend.at[mat, region], crecv.at[mat, region], at.twin)
+
+    def add_core(mat, group):
+        core_copy[mat][group].wait_recv()
+        region = pl.ds(group * Q, Q)
+        acc[mat, region] += crecv[mat, region].astype(jnp.float32)
+
+    def reduce_send(mat, name, base, size, place, target):
+        spot = pl.ds(place, size)
+        rsend[mat, spot] = acc[mat, pl.ds(base, size)].astype(jnp.bfloat16)
+        copy = at.push(rsend.at[mat, spot], rrecv.at[mat, spot], target)
+        moved[mat][name] = (copy, place, size)
+
+    def reduce_add(mat, name, base):
+        copy, place, size = moved[mat][name]
+        copy.wait_recv()
+        acc[mat, pl.ds(base, size)] += rrecv[mat, pl.ds(place, size)].astype(jnp.float32)
+
+    def product_tasks(mat):
+        multiply(mat, 3)
+        yield
+        multiply(mat, 2)
+        yield
+        add_core(mat, 3)
+        reduce_send(mat, "second", 3 * Q, Q, Q, far)
+        multiply(mat, 1)
+        yield
+        multiply(mat, 0)
+        add_core(mat, 2)
+        add_core(mat, 1)
+        reduce_send(mat, "first", (2 - core) * Q, Q, 0, far)
+        yield
+
+    def reduce_tasks(mat):
+        reduce_add(mat, "second", (1 + core) * Q)
+        reduce_send(mat, "near", (1 + core) * Q, Q, 2 * Q, near)
+        yield
+        add_core(mat, 0)
+        reduce_add(mat, "first", 0)
+        yield
+        reduce_add(mat, "near", 0)
+        for i in reversed(range(m - 2)):
+            reduce_send(mat, i, 2**i, 2**i, 3 * Q + Q - 2 ** (i + 1), at.partner[i])
+            yield
+            reduce_add(mat, i, 0)
+        mine = acc[mat, 0] / pods
+        own[mat, core] = mine
+        sfull[mat, 0, core] = mine.astype(jnp.bfloat16)
+        gather = Gather(at, sfull.at[mat])
+        gather.start(0)
+        own_copy = at.push(own.at[mat, core], own.at[mat, core], at.twin)
+        gather.swap("own", 0, 1)
+        yield
+        for i in range(m):
+            gather.step(i)
+            yield
+        own_copy.wait_recv()
+        for part, value in enumerate(terms(own[mat].reshape(rank, cols))):
+            start = own_spot + part * cols
+            grads[mat, row_spot:, start : start + cols] = value
+        for name in gather.swaps:
+            gather.swapped(name)
+
+        @pl.loop(0, n)
+        def _(q):
+            grads[mat, pl.ds(rows, rank), columns(q)] = sfull[mat, q].reshape(rank, cols)
+
+        yield
+
+    def drive(tasks, first_only=False):
+        live = list(tasks)
+        while live:
+            for task in list(live):
+                if next(task, StopIteration) is StopIteration:
+                    live.remove(task)
+                    if first_only and task is tasks[0]:
+                        return
+
+    round_product(0)
+    gate_product = product_tasks(0)
+    next(gate_product)
+    next(gate_product)
+    round_product(1)
+    gram = gram_tasks()
+    next(gram)
+    drive([gate_product])
+    gate_reduce = reduce_tasks(0)
+    up_reduce = reduce_tasks(1)
+    drive([product_tasks(1), gate_reduce, gram], first_only=True)
+    drive([gate_reduce, up_reduce, gram])
+
+
+def residual_kernel(
+    width, rank, rows, cols, grads,
+    next0_ref, next1_ref, factor0_ref, factor1_ref, r0_ref, r1_ref, left, made, sems,
+):
+    row_spot, own_spot, linv_spot = pack_of(rank, rows, cols)
+    tile = 256 if width % 256 == 0 else 128
+    steps = grads.shape[2] // width
+    for mat, (next_ref, factor_ref) in enumerate(
+        ((next0_ref, factor0_ref), (next1_ref, factor1_ref))
+    ):
+        def whole(start, size, step):
+            parts = [
+                grads[mat, row_spot:, start + k * step : start + k * step + size].astype(jnp.float32)
+                for k in range(3)
+            ]
+            return parts[0] + (parts[1] + parts[2])
+
+        inverse = whole(linv_spot, rank, 128)
+        next_ref[...] = jnp.dot(inverse, whole(own_spot, cols, cols), precision=HIGHEST)
+        product = grads[mat, row_spot:, :rows].astype(jnp.float32)
+        rows_t = jnp.dot(inverse, product, precision=HIGHEST)
+        factor_ref[...] = rows_t
+        mixed = lax.dot_general(inverse, rows_t, (((0,), (0,)), ((), ())), precision=HIGHEST).T
+        top = mixed.astype(jnp.bfloat16)
+        rest = (mixed - top.astype(jnp.float32)).astype(jnp.bfloat16)
+        left[mat] = jnp.concatenate([top, rest], axis=1)
+
+    def store(mat, i):
+        slot = i % 2
+        start = pl.multiple_of(i * width, 128)
+        return pltpu.make_async_copy(
+            made.at[mat, slot], (r0_ref, r1_ref)[mat].at[0, :, pl.ds(start, width)],
+            sems.at[mat, slot],
+        )
+
+    @pl.loop(0, steps)
+    def _(i):
+        for mat in range(2):
+            @pl.when(i >= 2)
+            def _():
+                store(mat, i - 2).wait()
+
+            for k in range(width // tile):
+                here = pl.ds(pl.multiple_of(i * width + k * tile, 128), tile)
+                block = grads[mat, rows : rows + rank, here]
+                product = jnp.dot(
+                    left[mat], jnp.concatenate([block, block], axis=0),
+                    preferred_element_type=jnp.float32,
+                )
+                made[mat, i % 2, :, k * tile : (k + 1) * tile] = (
+                    grads[mat, :rows, here].astype(jnp.float32) - product
+                ).astype(jnp.bfloat16)
+            store(mat, i).start()
+
+    for i in range(max(steps - 2, 0), steps):
+        for mat in range(2):
+            store(mat, i).wait()
+
+
+def fused(n, pods, grad_gate, grad_up, basis_gate, basis_up):
+    _, rows, full_cols = grad_gate.shape
+    rank, cols = basis_gate.shape
+    half = rank // 2
+    m = n.bit_length() - 1
+    vmem = pl.BlockSpec(memory_space=pltpu.VMEM)
+    anywhere = pl.BlockSpec(memory_space=pl.ANY)
+    f32, bf16 = jnp.float32, jnp.bfloat16
+    flops = 4 * rows * full_cols * rank
+
+    gather = 2 * (m + 1)
+    count = 2 * (gather + 1 + m + 4 + (m + 1) + gather + 2)
+    packed = pl.pallas_call(
+        functools.partial(forward_kernel, n, pods),
+        out_shape=pltpu.VMEM((2, rows + 2 * rank, full_cols), bf16),
+        in_specs=[anywhere, anywhere, vmem, vmem],
+        out_specs=vmem,
+        scratch_shapes=[
+            pltpu.VMEM((2, rank, rows), bf16),
+            pltpu.VMEM((2, n, 2, half, cols), bf16),
+            pltpu.VMEM((2, rows, rank), f32),
+            pltpu.VMEM((2, rank, rows), f32),
+            pltpu.VMEM((2, rank, rows), f32),
+            pltpu.VMEM((2, n, 2, half, cols), bf16),
+            pltpu.VMEM((2, n, half, cols), f32),
+            pltpu.VMEM((2, n, half, cols), bf16),
+            pltpu.VMEM((2, n, half, cols), bf16),
+            pltpu.VMEM((2, n, half, cols), bf16),
+            pltpu.VMEM((2, n, half, cols), bf16),
+            pltpu.VMEM((2, m + 1, rank, rank), f32),
+            pltpu.VMEM((2, m, rank, rank), f32),
+            pltpu.VMEM((2, 2, half, cols), f32),
+            pltpu.SemaphoreType.DMA((count,)),
+            pltpu.SemaphoreType.DMA((count,)),
+            pltpu.SemaphoreType.DMA((2 * n,)),
+        ],
+        compiler_params=pltpu.CompilerParams(
+            collective_id=0, has_side_effects=True, vmem_limit_bytes=20 * 2**20
+        ),
+        cost_estimate=pl.CostEstimate(
+            flops=2 * flops, bytes_accessed=4 * rows * full_cols, transcendentals=0
+        ),
+    )(grad_gate, grad_up, basis_gate, basis_up)
+
+    width = next(
+        w for w in (1024, 512, 256, 128) if full_cols % w == 0
+    )
+    next_gate, next_up, factor_gate, factor_up, resid_gate, resid_up = pl.pallas_call(
+        functools.partial(residual_kernel, width, rank, rows, cols),
+        out_shape=[
+            jax.ShapeDtypeStruct((rank, cols), f32),
+            jax.ShapeDtypeStruct((rank, cols), f32),
+            jax.ShapeDtypeStruct((rank, rows), f32),
+            jax.ShapeDtypeStruct((rank, rows), f32),
+            jax.ShapeDtypeStruct(grad_gate.shape, bf16),
+            jax.ShapeDtypeStruct(grad_up.shape, bf16),
+        ],
+        in_specs=[vmem],
+        out_specs=[vmem] * 4 + [anywhere] * 2,
+        scratch_shapes=[
+            pltpu.VMEM((2, rows, 2 * rank), bf16),
+            pltpu.VMEM((2, 2, rows, width), bf16),
+            pltpu.SemaphoreType.DMA((2, 2)),
+        ],
+        compiler_params=pltpu.CompilerParams(vmem_limit_bytes=20 * 2**20),
+        cost_estimate=pl.CostEstimate(
+            flops=flops, bytes_accessed=4 * rows * full_cols, transcendentals=0
+        ),
+    )(packed)
+    return next_gate, next_up, factor_gate.T, factor_up.T, resid_gate, resid_up
+
+
+def dispatch(grad_gate, grad_up, basis_gate, basis_up):
+    n = lax.axis_size("row")
+    pods = lax.axis_size("outer")
+    pod_part, rows, full_cols = grad_gate.shape
+    rank, cols = basis_gate.shape
+    fits = (
+        pods == 2 and pod_part == 1 and n >= 4 and n & (n - 1) == 0
+        and cols % 128 == 0 and rows % 128 == 0 and rank % 32 == 0
+        and 4 * rows * full_cols <= 32 * 2**20 and rows + 3 * cols + 384 <= full_cols
+        and rank <= 128
+    )
+    if fits:
+        return fused(n, pods, grad_gate, grad_up, basis_gate, basis_up)
+    return local(grad_gate, grad_up, basis_gate, basis_up)
+
+
 def solution(mesh):
     return jax.shard_map(
-        local,
+        dispatch,
         mesh=mesh,
         in_specs=(P("outer", "row", None), P("outer", "row", None), P(None, "row"), P(None, "row")),
         out_specs=(

time: 357 us -> 101 us (0.28)
  blocking collectives: 140 us -> 0 us
  Pallas kernels: 0 us -> 98.2 us
  matrix products: 94.2 us -> 0 us
  waiting for transfers between devices: 89.5 us -> 0 us
  between operations: 14.2 us -> 0.65 us
  other arithmetic: 13.4 us -> 0 us
    pallas_call x0 -> x2, Pallas kernels: none -> 98.2 us  [the longest x1 83.7 us: fused(): pl.pallas_call(functools.partial(forward_kernel, n, pods), out_shape=pltp...]
    psum x2 -> x0, waiting for transfers between devices: 89.4 us -> none  [the longest x1 60.4 us: local(): totals = lax.psum((products[0], products[1]), ('outer', 'row'))]
    dot_general x8 -> x0, matrix products: 88.8 us -> none  [the longest x1 28.1 us: local(): jnp.dot(factor_up, full_up, precision=lax.Precision.HIGHEST)]
    all_gather x2 -> x0, blocking collectives: 75.9 us -> none  [the longest x1 40.6 us: local(): lax.all_gather(basis_gate, 'row', axis=1, tiled=True)]
    psum x1 -> x0, blocking collectives: 64.6 us -> none  [local(): lax.psum((contract_rows(round_gate, round_gate), contract_rows(round_up,...]
    another operation x10 -> x0, other arithmetic: 13.4 us -> none  [the longest x4 6.17 us: forward_solve(): jax.scipy.linalg.solve_triangular(lower_matrix, right_hand, lower=True)]
    another operation x4 -> x0, matrix products: 5.45 us -> none  [forward_solve(): jax.scipy.linalg.solve_triangular(lower_matrix, right_hand, lower=True)]
  transfers between devices with their start and end apart: 2 -> 0, of which waited for: 2 -> 0; matrix products, arithmetic and copies ran while one was open for 4% -> 0% of each run, Pallas kernels for 0% -> 0%
where the time goes in v2:
time: 101 us; the launch traced here: 100 us
  Pallas kernels  98.2 us (97%)
  local copies, waits for them, and re-layouts  1.63 us (2%)
    pallas_call x1, Pallas kernels, fused(): pl.pallas_call(functools.partial(forward_kernel, n, pods), out_shape=pltp...  83.7 us
    pallas_call x1, Pallas kernels, fused(): pl.pallas_call(functools.partial(residual_kernel, width, rank, rows, cols...  14.5 us

profile of v2, /device:TPU:1, one launch (start us, length us, event | category | flops | bytes accessed | tf_op | source)
XLA Modules:
  0.0 100.5 jit_solution(8623098899861296847)
XLA Ops:
  0.6 0.0 copy-start
  0.6 0.8 copy-done
  1.5 0.0 copy-start.1
  1.5 0.8 copy-done.1
  2.3 83.7 %shard_map.91.grads = bf16[2,576,14336]{2,1,0:T(8,128)(2,1)S(1)} custom-call(bf16[1,512,14336]{2,1,0:T(8,128)(2,1)} %g0_ref.1, bf16[1,512,14336]{2,1,0:T(8,128)(2,1)} %g1_ref.1, bf16[32,896]{1,0:T(8,128)(2,1)S(1)} %copy-done, bf16[32,896]{1,0:T(8,128)(2,1)S(1)} %copy-done.1), custom_call_target="tpu_custom_call" | custom-call | flops 1879048192 | bytes 29360128 | tf_op jit(solution)/shard_map/pallas_call | solution.py:471
  85.9 14.5 %shard_map.92 = (f32[32,896]{1,0:T(8,128)}, f32[32,896]{1,0:T(8,128)}, f32[32,512]{1,0:T(8,128)}, f32[32,512]{1,0:T(8,128)}, bf16[1,512,14336]{2,1,0:T(8,128)(2,1)}, /*index=5*/bf16[1,512,14336]{2,1,0:T(8,128)(2,1)}) custom-call(bf16[2,576,14336]{2,1,0:T(8,128)(2,1)S(1)} %shard_map.91.grads), custom_call_target="tpu_custom_call" | custom-call | flops 939524096 | bytes 29360128 | tf_op jit(solution)/shard_map/pallas_call | solution.py:506
Async XLA Ops:
  0.6 0.8 copy-start
  1.5 0.8 copy-start.1

commit v3 on v2

--- a/solution.py
+++ b/solution.py
@@ -77,7 +77,10 @@
         self.slot_delta = [delta[m - 1 - i] for i in range(m - 2)] + [delta[0], delta[1]]
         self.near = {"row": self.me + (1 - self.core) * delta[0] + self.core * delta[1]}
         self.far = {"row": self.me + (1 - self.core) * delta[1] + self.core * delta[0]}
-        self.partner = [{"row": self.me + delta[m - 1 - i]} for i in range(m - 2)]
+        self.peers = [
+            {"row": self.me + sum(((p // 2**i) % 2) * delta[m - 1 - i] for i in range(m - 2))}
+            for p in range(self.Q)
+        ]
         self.twin = {"outer": 1 - self.core}
         self.sems = (send_sems, recv_sems)
         self.sent = []
@@ -90,7 +93,7 @@
 
     def greet(self):
         barrier = pltpu.get_barrier_semaphore()
-        targets = self.partner + [
+        targets = self.peers[1:] + [
             {"row": self.me + self.delta[0]}, {"row": self.me + self.delta[1]}, self.twin,
         ]
         for target in targets:
@@ -122,50 +125,51 @@
         )
         self.moves[name] = (copy, dst, size)
 
-    def start(self, i):
-        m, Q, core = self.at.m, self.at.Q, self.at.core
-        if i < m - 2:
-            self.go(i, 0, 2**i, 2**i, self.at.partner[i])
-        elif i == m - 2:
-            self.go("near", 0, (1 + core) * Q, Q, self.at.near)
-            self.go("far", 0, (2 - core) * Q, Q, self.at.far)
-        else:
-            self.go("last", (1 + core) * Q, 3 * Q, Q, self.at.far)
+    def start(self):
+        for p in range(1, self.at.Q):
+            self.go(p, 0, p, 1, self.at.peers[p])
+
+    def spread(self):
+        Q, core = self.at.Q, self.at.core
+        for p in range(1, Q):
+            self.moves[p][0].wait_recv()
+        self.go("near", 0, (1 + core) * Q, Q, self.at.near)
+        self.go("far", 0, (2 - core) * Q, Q, self.at.far)
+        self.swap("peers", 1, Q - 1)
+
+    def pass_on(self):
+        Q, core = self.at.Q, self.at.core
+        self.moves["near"][0].wait_recv()
+        self.go("last", (1 + core) * Q, 3 * Q, Q, self.at.far)
+        self.land("near")
+        self.land("far")
 
     def land(self, name):
         copy, dst, size = self.moves[name]
-        copy.wait_recv()
+        if name != "near":
+            copy.wait_recv()
         self.swap(name, dst, size)
 
     def swap(self, name, dst, size):
         region = self.ref.at[pl.ds(dst, size), self.at.core]
         self.swaps[name] = self.at.push(region, region, self.at.twin)
 
-    def swapped(self, name):
-        self.swaps[name].wait_recv()
-
-    def step(self, i):
-        m = self.at.m
-        if i < m - 2:
-            self.land(i)
-            self.start(i + 1)
-        elif i == m - 2:
-            self.land("near")
-            self.start(i + 1)
-            self.land("far")
-        else:
-            self.land("last")
+    def swapped(self, *names):
+        for name in names:
+            self.swaps[name].wait_recv()
 
 
 def forward_kernel(
     n, pods, g0_ref, g1_ref, b0_ref, b1_ref, grads,
     prt_ref, basis, pacc, ptsend, ptrecv, sfull, acc, csend, crecv, rsend, rrecv, gsend, grecv, own,
-    send_sems, recv_sems, g_sems,
+    send_sems, recv_sems, g_sems, b_sems,
 ):
     at = Place(n, send_sems, recv_sems)
-    copies = project_part(
+    upper = project_part(
         at, n, g0_ref, g1_ref, b0_ref, b1_ref, grads, basis, pacc, ptsend, ptrecv, g_sems,
-    )
+        b_sems,
+    )
+    copies = [next(upper)]
 
     def round_product(mat):
         copies[mat].wait_recv()
@@ -175,7 +179,7 @@
         gsend[mat, 0] = contract_cols(prt_ref[mat], prt_ref[mat])
 
     reduce_part(
-        at, n, pods, b0_ref.shape[1], round_product, grads, prt_ref,
+        at, n, pods, b0_ref.shape[1], upper, copies, round_product, grads, prt_ref,
         sfull, acc, csend, crecv, rsend, rrecv, gsend, grecv, own,
     )
     for copy in at.sent:
@@ -195,6 +199,7 @@
 
 def project_part(
     at, n, g0_ref, g1_ref, b0_ref, b1_ref, grads, basis, pacc, ptsend, ptrecv, g_sems,
+    b_sems,
 ):
     m, Q = at.m, at.Q
     rank, cols = b0_ref.shape
@@ -211,13 +216,24 @@
         )
 
     greeted = at.greet()
+    own = [
+        pltpu.make_async_copy(
+            basis_refs[mat].at[pl.ds(part * (rank // 2), rank // 2)], basis.at[mat, 0, part],
+            b_sems.at[2 * mat + part],
+        )
+        for mat in range(2)
+        for part in range(2)
+    ]
+    for copy in own:
+        copy.start()
     for mat in range(2):
         @pl.loop(0, n)
         def _(q):
             load(mat, q).start()
 
-        basis[mat, 0] = basis_refs[mat][...].reshape(2, rank // 2, cols)
         pacc[mat] = jnp.zeros(pacc.shape[1:], jnp.float32)
+    for copy in own:
+        copy.wait()
     greeted()
 
     def project(mat, base, size):
@@ -229,30 +245,41 @@
                 grads[mat, pl.ds(0, grad_refs[mat].shape[1]), columns(q)], basis[mat, q].reshape(rank, cols)
             )
 
-    gathers = [Gather(at, basis.at[mat]) for mat in range(2)]
-    for mat in range(2):
-        gathers[mat].start(0)
-    for mat in range(2):
-        project(mat, 0, 1)
-    for i in range(m):
-        for mat in range(2):
-            gathers[mat].step(i)
-        if 1 <= i <= m - 2:
-            for mat in range(2):
-                gathers[mat].swapped(i - 1)
-                project(mat, 2 ** (i - 1), 2 ** (i - 1))
-    copies = []
-    for mat in range(2):
-        for name in ("near", "far", "last"):
-            gathers[mat].swapped(name)
-        project(mat, Q, 3 * Q)
+    def exchange(mat):
         ptsend[mat] = pacc[mat].T
-        copies.append(at.push(ptsend.at[mat], ptrecv.at[mat], at.twin))
-    return copies
+        return at.push(ptsend.at[mat], ptrecv.at[mat], at.twin)
+
+    gate, up = (Gather(at, basis.at[mat]) for mat in range(2))
+    gate.start()
+    project(0, 0, 1)
+    gate.spread()
+    up.start()
+    gate.swapped("peers")
+    project(0, 1, Q - 1)
+    project(1, 0, 1)
+    gate.pass_on()
+    up.spread()
+    gate.swapped("near", "far")
+    project(0, Q, 2 * Q)
+    gate.land("last")
+    up.swapped("peers")
+    project(1, 1, Q - 1)
+    gate.swapped("last")
+    project(0, 3 * Q, Q)
+    yield exchange(0)
+    up.pass_on()
+    yield
+    up.land("last")
+    up.swapped("near", "far")
+    yield
+    project(1, Q, 2 * Q)
+    up.swapped("last")
+    project(1, 3 * Q, Q)
+    yield exchange(1)
 
 
 def reduce_part(
-    at, n, pods, cols, round_product, grads, prt_ref,
+    at, n, pods, cols, upper, copies, round_product, grads, prt_ref,
     sfull, acc, csend, crecv, rsend, rrecv, gsend, grecv, own,
 ):
     m, Q, core, near, far = at.m, at.Q, at.core, at.near, at.far
@@ -264,17 +291,29 @@
         return pl.ds(pl.multiple_of(at.block_of(q) * cols, 128), cols)
 
     def gram_tasks():
-        for k in range(m):
-            target = {"row": at.me + at.delta[m - 1 - k]}
-            copies = [at.push(gsend.at[mat, k], grecv.at[mat, k], target) for mat in range(2)]
+        spot = 0
+        for k, targets in enumerate(
+            (at.peers[1:], [{"row": at.me + at.delta[1]}], [{"row": at.me + at.delta[0]}])
+        ):
+            moves = [
+                [
+                    at.push(gsend.at[mat, k], grecv.at[mat, spot + i], target)
+                    for i, target in enumerate(targets)
+                ]
+                for mat in range(2)
+            ]
             yield
             for mat in range(2):
-                copies[mat].wait_recv()
-                gsend[mat, k + 1] = gsend[mat, k] + grecv[mat, k]
+                total = gsend[mat, k]
+                for i, move in enumerate(moves[mat]):
+                    move.wait_recv()
+                    total = total + grecv[mat, spot + i]
+                gsend[mat, k + 1] = total
+            spot += len(targets)
         sub = lax.broadcasted_iota(jnp.int32, (rank, 2 * rank), 0)
         lane = lax.broadcasted_iota(jnp.int32, (rank, 2 * rank), 1)
         unit = jnp.where(lane == sub + rank, 1.0, 0.0).astype(jnp.float32)[:, rank:]
-        systems = [jnp.concatenate([gsend[mat, m], unit], axis=1) for mat in range(2)]
+        systems = [jnp.concatenate([gsend[mat, 3], unit], axis=1) for mat in range(2)]
         for k in range(rank):
             for mat in range(2):
                 system = systems[mat]
@@ -346,27 +385,34 @@
         reduce_add(mat, "first", 0)
         yield
         reduce_add(mat, "near", 0)
-        for i in reversed(range(m - 2)):
-            reduce_send(mat, i, 2**i, 2**i, 3 * Q + Q - 2 ** (i + 1), at.partner[i])
-            yield
-            reduce_add(mat, i, 0)
+        rsend[mat, pl.ds(3 * Q, Q - 1)] = acc[mat, pl.ds(1, Q - 1)].astype(jnp.bfloat16)
+        for p in range(1, Q):
+            spot = pl.ds(3 * Q + p - 1, 1)
+            moved[mat][p] = (
+                at.push(rsend.at[mat, spot], rrecv.at[mat, spot], at.peers[p]), 3 * Q + p - 1, 1,
+            )
+        yield
+        for p in range(1, Q):
+            reduce_add(mat, p, 0)
         mine = acc[mat, 0] / pods
         own[mat, core] = mine
         sfull[mat, 0, core] = mine.astype(jnp.bfloat16)
         gather = Gather(at, sfull.at[mat])
-        gather.start(0)
+        gather.start()
         own_copy = at.push(own.at[mat, core], own.at[mat, core], at.twin)
         gather.swap("own", 0, 1)
         yield
-        for i in range(m):
-            gather.step(i)
-            yield
+        gather.spread()
+        yield
+        gather.pass_on()
+        yield
+        gather.land("last")
+        yield
         own_copy.wait_recv()
         for part, value in enumerate(terms(own[mat].reshape(rank, cols))):
             start = own_spot + part * cols
             grads[mat, row_spot:, start : start + cols] = value
-        for name in gather.swaps:
-            gather.swapped(name)
+        gather.swapped(*gather.swaps)
 
         @pl.loop(0, n)
         def _(q):
@@ -386,12 +432,17 @@
     round_product(0)
     gate_product = product_tasks(0)
     next(gate_product)
+    next(upper)
     next(gate_product)
+    next(gate_product)
+    next(upper)
+    next(gate_product)
+    copies.append(next(upper))
+    gate_reduce = reduce_tasks(0)
+    next(gate_reduce)
     round_product(1)
     gram = gram_tasks()
     next(gram)
-    drive([gate_product])
-    gate_reduce = reduce_tasks(0)
     up_reduce = reduce_tasks(1)
     drive([product_tasks(1), gate_reduce, gram], first_only=True)
     drive([gate_reduce, up_reduce, gram])
@@ -460,18 +511,18 @@
     _, rows, full_cols = grad_gate.shape
     rank, cols = basis_gate.shape
     half = rank // 2
-    m = n.bit_length() - 1
     vmem = pl.BlockSpec(memory_space=pltpu.VMEM)
     anywhere = pl.BlockSpec(memory_space=pl.ANY)
+    hbm = pl.BlockSpec(memory_space=pltpu.HBM)
     f32, bf16 = jnp.float32, jnp.bfloat16
     flops = 4 * rows * full_cols * rank
 
-    gather = 2 * (m + 1)
-    count = 2 * (gather + 1 + m + 4 + (m + 1) + gather + 2)
+    gather = (n // 4 - 1) + 3 + 4
+    count = 2 * (gather + 1 + (n // 4 + 1) + 4 + (n // 4 + 2) + gather + 2)
     packed = pl.pallas_call(
         functools.partial(forward_kernel, n, pods),
         out_shape=pltpu.VMEM((2, rows + 2 * rank, full_cols), bf16),
-        in_specs=[anywhere, anywhere, vmem, vmem],
+        in_specs=[anywhere, anywhere, hbm, hbm],
         out_specs=vmem,
         scratch_shapes=[
             pltpu.VMEM((2, rank, rows), bf16),
@@ -485,12 +536,13 @@
             pltpu.VMEM((2, n, half, cols), bf16),
             pltpu.VMEM((2, n, half, cols), bf16),
             pltpu.VMEM((2, n, half, cols), bf16),
-            pltpu.VMEM((2, m + 1, rank, rank), f32),
-            pltpu.VMEM((2, m, rank, rank), f32),
+            pltpu.VMEM((2, 4, rank, rank), f32),
+            pltpu.VMEM((2, n // 4 + 1, rank, rank), f32),
             pltpu.VMEM((2, 2, half, cols), f32),
             pltpu.SemaphoreType.DMA((count,)),
             pltpu.SemaphoreType.DMA((count,)),
             pltpu.SemaphoreType.DMA((2 * n,)),
+            pltpu.SemaphoreType.DMA((4,)),
         ],
         compiler_params=pltpu.CompilerParams(
             collective_id=0, has_side_effects=True, vmem_limit_bytes=20 * 2**20

time: 101 us -> 96.2 us (0.952)
  Pallas kernels: 98.2 us -> 93.7 us
    pallas_call x1, Pallas kernels: 83.7 us -> 79.2 us  [fused(): pl.pallas_call(functools.partial(forward_kernel, n, pods), out_shape=pltp...]
where the time goes in v3:
time: 96.2 us; the launch traced here: 96 us
  Pallas kernels  93.7 us (97%)
  local copies, waits for them, and re-layouts  1.63 us (2%)
    pallas_call x1, Pallas kernels, fused(): pl.pallas_call(functools.partial(forward_kernel, n, pods), out_shape=pltp...  79.2 us
    pallas_call x1, Pallas kernels, fused(): pl.pallas_call(functools.partial(residual_kernel, width, rank, rows, cols...  14.5 us

profile of v3, /device:TPU:1, one launch (start us, length us, event | category | flops | bytes accessed | tf_op | source)
XLA Modules:
  0.0 96.0 jit_solution(1643571034781223857)
XLA Ops:
  0.6 0.0 copy-start
  0.6 0.8 copy-done
  1.5 0.0 copy-start.1
  1.5 0.8 copy-done.1
  2.3 79.2 %shard_map.91.grads = bf16[2,576,14336]{2,1,0:T(8,128)(2,1)S(1)} custom-call(bf16[1,512,14336]{2,1,0:T(8,128)(2,1)} %g0_ref.1, bf16[1,512,14336]{2,1,0:T(8,128)(2,1)} %g1_ref.1, bf16[32,896]{1,0:T(8,128)(2,1)S(1)} %copy-done, bf16[32,896]{1,0:T(8,128)(2,1)S(1)} %copy-done.1), custom_call_target="tpu_custom_call" | custom-call | flops 1879048192 | bytes 29360128 | tf_op jit(solution)/shard_map/pallas_call | solution.py:522
  81.5 14.5 %shard_map.92 = (f32[32,896]{1,0:T(8,128)}, f32[32,896]{1,0:T(8,128)}, f32[32,512]{1,0:T(8,128)}, f32[32,512]{1,0:T(8,128)}, bf16[1,512,14336]{2,1,0:T(8,128)(2,1)}, /*index=5*/bf16[1,512,14336]{2,1,0:T(8,128)(2,1)}) custom-call(bf16[2,576,14336]{2,1,0:T(8,128)(2,1)S(1)} %shard_map.91.grads), custom_call_target="tpu_custom_call" | custom-call | flops 939524096 | bytes 29360128 | tf_op jit(solution)/shard_map/pallas_call | solution.py:558
Async XLA Ops:
  0.6 0.8 copy-start
  1.5 0.8 copy-start.1

commit v4 on v3

--- a/solution.py
+++ b/solution.py
@@ -420,14 +420,12 @@
 
         yield
 
-    def drive(tasks, first_only=False):
+    def drive(tasks):
         live = list(tasks)
         while live:
             for task in list(live):
                 if next(task, StopIteration) is StopIteration:
                     live.remove(task)
-                    if first_only and task is tasks[0]:
-                        return
 
     round_product(0)
     gate_product = product_tasks(0)
@@ -444,7 +442,12 @@
     gram = gram_tasks()
     next(gram)
     up_reduce = reduce_tasks(1)
-    drive([product_tasks(1), gate_reduce, gram], first_only=True)
+    up_product = product_tasks(1)
+    next(up_product)
+    next(up_product)
+    next(gate_reduce)
+    next(up_product)
+    next(up_product)
     drive([gate_reduce, up_reduce, gram])
 
 
@@ -516,6 +519,9 @@
     hbm = pl.BlockSpec(memory_space=pltpu.HBM)
     f32, bf16 = jnp.float32, jnp.bfloat16
     flops = 4 * rows * full_cols * rank
+
+    def in_hbm(array):
+        return pltpu.with_memory_space_constraint(array, pltpu.HBM)
 
     gather = (n // 4 - 1) + 3 + 4
     count = 2 * (gather + 1 + (n // 4 + 1) + 4 + (n // 4 + 2) + gather + 2)
@@ -550,7 +556,7 @@
         cost_estimate=pl.CostEstimate(
             flops=2 * flops, bytes_accessed=4 * rows * full_cols, transcendentals=0
         ),
-    )(grad_gate, grad_up, basis_gate, basis_up)
+    )(grad_gate, grad_up, in_hbm(basis_gate), in_hbm(basis_up))
 
     width = next(
         w for w in (1024, 512, 256, 128) if full_cols % w == 0

time: 96.2 us -> 84.6 us (0.88)
  Pallas kernels: 93.7 us -> 83.8 us
  local copies, waits for them, and re-layouts: 1.63 us -> 0 us
    pallas_call x1, Pallas kernels: 79.2 us -> 69.3 us  [fused(): pl.pallas_call(functools.partial(forward_kernel, n, pods), out_shape=pltp...]
    unnamed x4 -> x0, local copies, waits for them, and re-layouts: 1.63 us -> none
where the time goes in v4:
time: 84.6 us; the launch traced here: 84.5 us
  Pallas kernels  83.8 us (99%)
    pallas_call x1, Pallas kernels, fused(): pl.pallas_call(functools.partial(forward_kernel, n, pods), out_shape=pltp...  69.3 us
    pallas_call x1, Pallas kernels, fused(): pl.pallas_call(functools.partial(residual_kernel, width, rank, rows, cols...  14.5 us

profile of v4, /device:TPU:1, one launch (start us, length us, event | category | flops | bytes accessed | tf_op | source)
XLA Modules:
  0.0 84.5 jit_solution(13953435845621127005)
XLA Ops:
  0.6 69.3 %shard_map.91.grads = bf16[2,576,14336]{2,1,0:T(8,128)(2,1)S(1)} custom-call(bf16[1,512,14336]{2,1,0:T(8,128)(2,1)} %g0_ref.1, bf16[1,512,14336]{2,1,0:T(8,128)(2,1)} %g1_ref.1, bf16[32,896]{1,0:T(8,128)(2,1)} %b0_ref.1, bf16[32,896]{1,0:T(8,128)(2,1)} %b1_ref.1), custom_call_target="tpu_custom_call" | custom-call | flops 1879048192 | bytes 29360128 | tf_op jit(solution)/shard_map/pallas_call | solution.py:528
  69.9 14.5 %shard_map.92 = (f32[32,896]{1,0:T(8,128)}, f32[32,896]{1,0:T(8,128)}, f32[32,512]{1,0:T(8,128)}, f32[32,512]{1,0:T(8,128)}, bf16[1,512,14336]{2,1,0:T(8,128)(2,1)}, /*index=5*/bf16[1,512,14336]{2,1,0:T(8,128)(2,1)}) custom-call(bf16[2,576,14336]{2,1,0:T(8,128)(2,1)S(1)} %shard_map.91.grads), custom_call_target="tpu_custom_call" | custom-call | flops 939524096 | bytes 29360128 | tf_op jit(solution)/shard_map/pallas_call | solution.py:564
